TPU v7x, 32 devices: a whole 2x2x4 slice. The times are simulated.
32 devices in a mesh: row: 4 (over y, x), col: 8 (over z, core).
Axes of the slice: x: 2, y: 2, z: 4, core: 2. Of those that a mesh axis runs over, the one named last changes fastest.
Arguments:
- upper_stored: bfloat16 [3072, 3072], P('row', 'col'), may hold values from -6 to 6
- block_cells: int32 [48, 3], replicated, may hold values from 0 to 15
Outputs:
- purified: bfloat16 [3072, 3072], P('row', 'col')
Inputs may be any that keep to these rules, and one draw needn't show every extreme that they name: `block_cells`: integer cell coordinates of each atom block on a periodic lattice of 16 cells a side.
All inputs are finite; a program needn't handle non-finite values.
Results may differ from a plain program's by a relative error of at most 0.0067.
Values may be sent and summed in bfloat16 or wider, within the bound.
A program may use at most 64 MiB of HBM per device.

v0:
```python
import math

import jax
import jax.numpy as jnp
from jax import lax
from jax.sharding import PartitionSpec as P

BLK = 64
BOX = 16
NEAR = 40
FAR = 90


def shifted_2(array, axis, by):
    length = lax.axis_size(axis)
    return lax.ppermute(array, axis, [(i, (i + by) % length) for i in range(length)])


def partner(value, axis, bit):
    mask = 2**bit
    pairs = [(source, source ^ mask) for source in range(lax.axis_size(axis))]
    return lax.ppermute(value, axis, pairs)


def cell_mask(block_cells, row_start, row_count, col_start, col_count, bound_sq):
    row_cells = lax.dynamic_slice_in_dim(block_cells, row_start, row_count, 0)
    col_cells = lax.dynamic_slice_in_dim(block_cells, col_start, col_count, 0)
    offset_abs = jnp.abs(row_cells[:, None, :] - col_cells[None, :, :])
    wrapped = jnp.minimum(offset_abs, BOX - offset_abs)
    return jnp.sum(wrapped * wrapped, axis=2) <= bound_sq


def block_keep(matrix_tile, keep_mask):
    row_count, col_count = matrix_tile.shape
    row_blocks, col_blocks = keep_mask.shape
    shaped = matrix_tile.reshape(
        row_blocks, row_count // row_blocks, col_blocks, col_count // col_blocks
    )
    kept = jnp.where(keep_mask[:, None, :, None], shaped, jnp.zeros_like(shaped))
    return kept.reshape(row_count, col_count)


def own_part(matrix_tile, layer_bit, half_width):
    return jnp.where(layer_bit == 0, matrix_tile[:, :half_width], matrix_tile[:, half_width:])


def partner_part(matrix_tile, layer_bit, half_width):
    return jnp.where(layer_bit == 0, matrix_tile[:, half_width:], matrix_tile[:, :half_width])


def join_halves(own_piece, partner_piece, layer_bit):
    first_order = jnp.concatenate([own_piece, partner_piece], 1)
    second_order = jnp.concatenate([partner_piece, own_piece], 1)
    return jnp.where(layer_bit == 0, first_order, second_order)


def skew_left(operand, row_id, layer_bit, grid_size):
    steps_wanted = (row_id + layer_bit * (grid_size // 2)) % grid_size
    for bit_pos in range((grid_size - 1).bit_length()):
        shifted = shifted_2(operand, "col", -(2 << bit_pos))
        operand = jnp.where((steps_wanted >> bit_pos) % 2 == 1, shifted, operand)
    return operand


def skew_right(operand, tile_col, layer_bit, grid_size):
    steps_wanted = (tile_col + layer_bit * (grid_size // 2)) % grid_size
    for bit_pos in range((grid_size - 1).bit_length()):
        shifted = shifted_2(operand, "row", -(1 << bit_pos))
        operand = jnp.where((steps_wanted >> bit_pos) % 2 == 1, shifted, operand)
    return operand


def cannon_half(left, right, grid_size):
    running = jnp.zeros((left.shape[0], right.shape[1]), jnp.float32)
    for section in range(grid_size // 2):
        running = running + jnp.dot(left, right, preferred_element_type=jnp.float32)
        if section + 1 < grid_size // 2:
            left = shifted_2(left, "col", -2)
            right = shifted_2(right, "row", -1)
    return running


def per_device(upper_stored, block_cells):
    grid_size = lax.axis_size("row")
    row_id = lax.axis_index("row")
    col_id = lax.axis_index("col")
    layer_bit = col_id % 2
    tile_col = col_id // 2
    tile_side, half_width = upper_stored.shape
    order_total = tile_side * grid_size
    tile_blocks = tile_side // BLK
    half_blocks = half_width // BLK
    slab_width = half_width // grid_size
    stacked = lax.all_to_all(
        lax.all_to_all(upper_stored, "row", split_axis=1, concat_axis=0, tiled=True),
        "col",
        split_axis=0,
        concat_axis=1,
        tiled=True,
    )
    gathered = lax.all_to_all(stacked.T, "row", split_axis=0, concat_axis=0, tiled=True)
    mirrored = (
        gathered.reshape(grid_size, 2, slab_width, half_width)
        .transpose(1, 0, 2, 3)
        .reshape(tile_side, half_width)
    )
    global_rows = row_id * tile_side + lax.broadcasted_iota(jnp.int32, (tile_side, half_width), 0)
    global_cols = col_id * half_width + lax.broadcasted_iota(jnp.int32, (tile_side, half_width), 1)
    symmetric = jnp.where(global_rows <= global_cols, upper_stored, mirrored)
    near_own = cell_mask(
        block_cells, row_id * tile_blocks, tile_blocks, col_id * half_blocks, half_blocks, NEAR
    )
    diagonal = jnp.where(global_rows == global_cols, 0.5, 0.0).astype(jnp.float32)
    value_scale = 2.0 / math.sqrt(order_total)
    own_density = block_keep(
        diagonal + value_scale * symmetric.astype(jnp.float32), near_own
    ).astype(jnp.bfloat16)
    partner_density = partner(own_density, "col", 0)
    density = join_halves(own_density, partner_density, layer_bit)
    right_start = skew_right(density, tile_col, layer_bit, grid_size)
    left_start = skew_left(density, row_id, layer_bit, grid_size)
    running = cannon_half(left_start, right_start, grid_size)
    far_full = cell_mask(
        block_cells, row_id * tile_blocks, tile_blocks, tile_col * tile_blocks, tile_blocks, FAR
    )
    partner_running = partner(running, "col", 0)
    square = block_keep(running + partner_running, far_full)
    square_low = square.astype(jnp.bfloat16)
    own_square = own_part(square, layer_bit, half_width)
    right_again = skew_right(density, tile_col, layer_bit, grid_size)
    left_again = skew_left(square_low, row_id, layer_bit, grid_size)
    cubic_running = cannon_half(left_again, right_again, grid_size)
    received_cubic = partner(partner_part(cubic_running, layer_bit, half_width), "col", 0)
    cubic = own_part(cubic_running, layer_bit, half_width) + received_cubic
    return block_keep(3.0 * own_square - 2.0 * cubic, near_own).astype(jnp.bfloat16)


def solution(mesh):
    return jax.shard_map(
        per_device,
        mesh=mesh,
        in_specs=(P("row", "col"), P()),
        out_specs=P("row", "col"),
        check_vma=False,
    )
```

profile of v0, /device:TPU:7, one launch (start us, length us, event | category | flops | bytes accessed | tf_op | source)
XLA Modules:
  0.0 294.3 jit_solution(14228180282946210902)
XLA Ops:
  0.0 1.3 copy.24
  1.3 10.1 %all_to_all.44 = bf16[768,4,96]{0,2,1:T(8,128)(2,1)S(1)} all-to-all(bf16[768,4,96]{0,2,1:T(8,128)(2,1)S(1)} %bitcast.26), channel_id=1, replica_groups=mesh['row'=4,'col'=8] {'row'}, dimensions={1} | all-to-all | bytes 1179648 | tf_op jit(solution)/shard_map/all_to_all | solution.py:95
  11.4 0.5 copy.25
  11.9 0.2 all_to_all.35
  12.0 0.9 copy.26
  12.9 6.7 %all-to-all-start.1 = ((bf16[8,384,96]{1,2,0:T(8,128)(2,1)}), bf16[8,384,96]{1,2,0:T(8,128)(2,1)}, u32[]{:S(2)}, u32[]{:S(2)}) async-start(bf16[8,384,96]{1,2,0:T(8,128)(2,1)} %copy.26), calls=%async_computation.1 | async-start | bytes 1179648 | tf_op jit(solution)/shard_map/all_to_all | solution.py:94
  19.8 15.8 %all-to-all-done.1 = bf16[8,384,96]{1,2,0:T(8,128)(2,1)} async-done(((bf16[8,384,96]{1,2,0:T(8,128)(2,1)}), bf16[8,384,96]{1,2,0:T(8,128)(2,1)}, u32[]{:S(2)}, u32[]{:S(2)}) %all-to-all-start.1) | async-done | bytes 589856 | tf_op jit(solution)/shard_map/all_to_all | solution.py:94
  35.6 5.4 %all-to-all-start.2 = ((bf16[4,192,384]{2,1,0:T(8,128)(2,1)}), bf16[4,192,384]{2,1,0:T(8,128)(2,1)S(1)}, u32[]{:S(2)}, u32[]{:S(2)}) async-start(bf16[4,192,384]{2,1,0:T(8,128)(2,1)} %bitcast.5), calls=%async_computation.2 | async-start | bytes 1179648 | tf_op jit(solution)/shard_map/all_to_all | solution.py:101
  41.1 0.3 broadcast_in_dim.41
  41.4 1.0 broadcast_in_dim.42
  42.4 5.3 %all-to-all-done.2 = bf16[4,192,384]{2,1,0:T(8,128)(2,1)S(1)} async-done(((bf16[4,192,384]{2,1,0:T(8,128)(2,1)}), bf16[4,192,384]{2,1,0:T(8,128)(2,1)S(1)}, u32[]{:S(2)}, u32[]{:S(2)}) %all-to-all-start.2) | async-done | bytes 589856 | tf_op jit(solution)/shard_map/all_to_all | solution.py:101
  47.8 0.5 select_convert_fusion
  48.3 1.7 collective-permute-start
  50.1 1.6 collective-permute-done
  51.7 0.3 maximum_select_fusion
  52.0 1.3 collective-permute-start.3
  53.3 1.4 collective-permute-start.1
  54.7 25.4 %collective-permute-done.3 = bf16[768,768]{1,0:T(8,128)(2,1)S(1)} collective-permute-done((bf16[768,768]{1,0:T(8,128)(2,1)S(1)}, bf16[768,768]{1,0:T(8,128)(2,1)S(1)}, u32[]{:S(2)}, u32[]{:S(2)}) %collective-permute-start.3) | collective-permute-done | bytes 1179680 | tf_op jit(solution)/shard_map/ppermute | solution.py:16
  80.1 1.0 copy-done.3
  81.1 1.5 broadcast_select_fusion
  82.6 1.3 collective-permute-start.4
  83.9 25.2 %collective-permute-done.4 = bf16[768,768]{1,0:T(8,128)(2,1)} collective-permute-done((bf16[768,768]{1,0:T(8,128)(2,1)S(1)}, bf16[768,768]{1,0:T(8,128)(2,1)}, u32[]{:S(2)}, u32[]{:S(2)}) %collective-permute-start.4) | collective-permute-done | bytes 1179680 | tf_op jit(solution)/shard_map/ppermute | solution.py:16
  109.0 1.4 broadcast_select_fusion.1
  110.5 26.9 %collective-permute-done.2 = bf16[768,768]{1,0:T(8,128)(2,1)S(1)} collective-permute-done((bf16[768,768]{1,0:T(8,128)(2,1)S(1)}, bf16[768,768]{1,0:T(8,128)(2,1)S(1)}, u32[]{:S(2)}, u32[]{:S(2)}) %collective-permute-start.2) | collective-permute-done | bytes 1179680 | tf_op jit(solution)/shard_map/ppermute | solution.py:16
  137.4 0.1 broadcast_select_fusion.5
  137.6 1.4 collective-permute-start.5
  139.0 25.6 %collective-permute-done.5 = bf16[768,768]{1,0:T(8,128)(2,1)S(1)} collective-permute-done((bf16[768,768]{1,0:T(8,128)(2,1)S(1)}, bf16[768,768]{1,0:T(8,128)(2,1)S(1)}, u32[]{:S(2)}, u32[]{:S(2)}) %collective-permute-start.5) | collective-permute-done | bytes 1179680 | tf_op jit(solution)/shard_map/ppermute | solution.py:16
  164.7 1.1 fusion.9
  165.8 2.5 convolution_add_fusion.1
  168.3 1.3 collective-permute-start.7
  169.7 0.5 broadcast_in_dim.43
  170.2 2.2 broadcast_in_dim.44
  172.4 1.7 collective-permute-done.7
  174.1 2.8 fusion.8
  176.9 3.2 %collective-permute-start.8 = (bf16[768,768]{1,0:T(8,128)(2,1)S(1)}, bf16[768,768]{1,0:T(8,128)(2,1)S(1)}, u32[]{:S(2)}, u32[]{:S(2)}) collective-permute-start(bf16[768,768]{1,0:T(8,128)(2,1)S(1)} %get-tuple-element.5), channel_id=1, source_target_pairs={{0,6},{1,7},{2,0},{3,1},{4,2},{5,3},{6,4},{7,5},{8,14},{9,15},{10,... | collective-permute-start | bytes 3538952 | tf_op jit(solution)/shard_map/ppermute | solution.py:16
  180.2 25.0 %collective-permute-done.8 = bf16[768,768]{1,0:T(8,128)(2,1)S(1)} collective-permute-done((bf16[768,768]{1,0:T(8,128)(2,1)S(1)}, bf16[768,768]{1,0:T(8,128)(2,1)S(1)}, u32[]{:S(2)}, u32[]{:S(2)}) %collective-permute-start.8) | collective-permute-done | bytes 1179680 | tf_op jit(solution)/shard_map/ppermute | solution.py:16
  205.2 0.2 broadcast_select_fusion.2
  205.3 1.4 collective-permute-start.9
  206.7 51.1 %collective-permute-done.9 = bf16[768,768]{1,0:T(8,128)(2,1)S(1)} collective-permute-done((bf16[768,768]{1,0:T(8,128)(2,1)S(1)}, bf16[768,768]{1,0:T(8,128)(2,1)S(1)}, u32[]{:S(2)}, u32[]{:S(2)}) %collective-permute-start.9) | collective-permute-done | bytes 1179680 | tf_op jit(solution)/shard_map/ppermute | solution.py:16
  257.8 0.1 broadcast_select_fusion.4
  258.0 3.9 %collective-permute-start.10 = (bf16[768,768]{1,0:T(8,128)(2,1)S(1)}, bf16[768,768]{1,0:T(8,128)(2,1)S(1)}, u32[]{:S(2)}, u32[]{:S(2)}) collective-permute-start(bf16[768,768]{1,0:T(8,128)(2,1)S(1)} %broadcast_select_fusion.4), channel_id=1, source_target_pairs={{0,6},{1,7},{2,0},{3,1},{4,2},{5,3},{6,4},{7,5},{8,14},{9,15},{10,... | collective-permute-start | bytes 3538952 | tf_op jit(solution)/shard_map/ppermute | solution.py:16
  261.9 24.8 %collective-permute-done.10 = bf16[768,768]{1,0:T(8,128)(2,1)S(1)} collective-permute-done((bf16[768,768]{1,0:T(8,128)(2,1)S(1)}, bf16[768,768]{1,0:T(8,128)(2,1)S(1)}, u32[]{:S(2)}, u32[]{:S(2)}) %collective-permute-start.10) | collective-permute-done | bytes 1179680 | tf_op jit(solution)/shard_map/ppermute | solution.py:16
  286.7 1.1 fusion.10
  287.8 1.1 convolution_add_fusion
  288.9 0.1 slice_select_fusion.1
  289.1 1.4 collective-permute-start.11
  290.5 2.5 collective-permute-done.11
  293.0 1.3 fusion.3
  (27 shorter events, 0.6 us)
Async XLA Ops:
  12.0 7.6 %copy-start.6 = (s32[48,3]{0,1:T(4,128)S(1)}, s32[48,3]{0,1:T(4,128)}, u32[]{:S(2)}) copy-start(s32[48,3]{0,1:T(4,128)} %param.3) | copy-start | bytes 1732
  12.9 22.7 %all-to-all-start.1 = ((bf16[8,384,96]{1,2,0:T(8,128)(2,1)}), bf16[8,384,96]{1,2,0:T(8,128)(2,1)}, u32[]{:S(2)}, u32[]{:S(2)}) async-start(bf16[8,384,96]{1,2,0:T(8,128)(2,1)} %copy.26), calls=%async_computation.1 | async-start | bytes 1179648 | tf_op jit(solution)/shard_map/all_to_all | solution.py:94
  35.6 12.1 %all-to-all-start.2 = ((bf16[4,192,384]{2,1,0:T(8,128)(2,1)}), bf16[4,192,384]{2,1,0:T(8,128)(2,1)S(1)}, u32[]{:S(2)}, u32[]{:S(2)}) async-start(bf16[4,192,384]{2,1,0:T(8,128)(2,1)} %bitcast.5), calls=%async_computation.2 | async-start | bytes 1179648 | tf_op jit(solution)/shard_map/all_to_all | solution.py:101
  41.3 6.4 %copy-start.2 = (bf16[768,384]{1,0:T(8,128)(2,1)S(1)}, bf16[768,384]{1,0:T(8,128)(2,1)}, u32[]{:S(2)}) copy-start(bf16[768,384]{1,0:T(8,128)(2,1)} %param.2) | copy-start | bytes 1769476
  42.4 5.9 %copy-start = (pred[768,384]{1,0:T(8,128)(4,1)}, pred[768,384]{1,0:T(8,128)(4,1)S(1)}, u32[]{:S(2)}) copy-start(pred[768,384]{1,0:T(8,128)(4,1)S(1)} %broadcast_in_dim.42) | copy-start | bytes 884740
  48.3 3.4 %collective-permute-start = (bf16[768,384]{1,0:T(8,128)(2,1)S(1)}, bf16[768,384]{1,0:T(8,128)(2,1)S(1)}, u32[]{:S(2)}, u32[]{:S(2)}) collective-permute-start(bf16[768,384]{1,0:T(8,128)(2,1)S(1)} %select_convert_fusion), channel_id=1, source_target_pairs={{0,1},{1,0},{2,3},{3,2},{4,5},{5,4},{6,7},{7,6},{8,9},{9,8},{10,11... | collective-permute-start | bytes 1769480 | tf_op jit(solution)/shard_map/ppermute | solution.py:22
  52.0 28.1 %collective-permute-start.3 = (bf16[768,768]{1,0:T(8,128)(2,1)S(1)}, bf16[768,768]{1,0:T(8,128)(2,1)S(1)}, u32[]{:S(2)}, u32[]{:S(2)}) collective-permute-start(bf16[768,768]{1,0:T(8,128)(2,1)S(1)} %maximum_select_fusion), channel_id=1, source_target_pairs={{0,24},{8,0},{16,8},{24,16},{1,25},{9,1},{17,9},{25,17},{2,26},{10... | collective-permute-start | bytes 3538952 | tf_op jit(solution)/shard_map/ppermute | solution.py:16
  53.3 27.9 %collective-permute-start.1 = (bf16[768,768]{1,0:T(8,128)(2,1)S(1)}, bf16[768,768]{1,0:T(8,128)(2,1)}, u32[]{:S(2)}, u32[]{:S(2)}) collective-permute-start(bf16[768,768]{1,0:T(8,128)(2,1)S(1)} %maximum_select_fusion), channel_id=1, source_target_pairs={{0,6},{1,7},{2,0},{3,1},{4,2},{5,3},{6,4},{7,5},{8,14},{9,15},{10,... | collective-permute-start | bytes 3538952 | tf_op jit(solution)/shard_map/ppermute | solution.py:16
  80.1 1.0 copy-start.3
  82.6 26.4 %collective-permute-start.4 = (bf16[768,768]{1,0:T(8,128)(2,1)S(1)}, bf16[768,768]{1,0:T(8,128)(2,1)}, u32[]{:S(2)}, u32[]{:S(2)}) collective-permute-start(bf16[768,768]{1,0:T(8,128)(2,1)S(1)} %get-tuple-element.7), channel_id=1, source_target_pairs={{0,16},{8,24},{16,0},{24,8},{1,17},{9,25},{17,1},{25,9},{2,18},{10... | collective-permute-start | bytes 3538952 | tf_op jit(solution)/shard_map/ppermute | solution.py:16
  83.9 53.6 %collective-permute-start.2 = (bf16[768,768]{1,0:T(8,128)(2,1)S(1)}, bf16[768,768]{1,0:T(8,128)(2,1)S(1)}, u32[]{:S(2)}, u32[]{:S(2)}) collective-permute-start(bf16[768,768]{1,0:T(8,128)(2,1)S(1)} %get-tuple-element.8), channel_id=1, source_target_pairs={{0,4},{1,5},{2,6},{3,7},{4,0},{5,1},{6,2},{7,3},{8,12},{9,13},{10,... | collective-permute-start | bytes 3538952 | tf_op jit(solution)/shard_map/ppermute | solution.py:16
  110.4 55.3 %copy-start.4 = (bf16[768,768]{1,0:T(8,128)(2,1)}, bf16[768,768]{1,0:T(8,128)(2,1)S(1)}, u32[]{:S(2)}) copy-start(bf16[768,768]{1,0:T(8,128)(2,1)S(1)} %broadcast_select_fusion.1) | copy-start | bytes 3538948
  110.5 28.6 %collective-permute-start.6 = (bf16[768,768]{1,0:T(8,128)(2,1)S(1)}, bf16[768,768]{1,0:T(8,128)(2,1)S(1)}, u32[]{:S(2)}, u32[]{:S(2)}) collective-permute-start(bf16[768,768]{1,0:T(8,128)(2,1)S(1)} %broadcast_select_fusion.1), channel_id=1, source_target_pairs={{0,24},{8,0},{16,8},{24,16},{1,25},{9,1},{17,9},{25,17},{2,26},{10... | collective-permute-start | bytes 3538952 | tf_op jit(solution)/shard_map/ppermute | solution.py:16
  137.6 27.1 %collective-permute-start.5 = (bf16[768,768]{1,0:T(8,128)(2,1)S(1)}, bf16[768,768]{1,0:T(8,128)(2,1)S(1)}, u32[]{:S(2)}, u32[]{:S(2)}) collective-permute-start(bf16[768,768]{1,0:T(8,128)(2,1)S(1)} %broadcast_select_fusion.5), channel_id=1, source_target_pairs={{0,6},{1,7},{2,0},{3,1},{4,2},{5,3},{6,4},{7,5},{8,14},{9,15},{10,... | collective-permute-start | bytes 3538952 | tf_op jit(solution)/shard_map/ppermute | solution.py:16
  168.3 5.8 %collective-permute-start.7 = (f32[768,768]{1,0:T(8,128)}, f32[768,768]{1,0:T(8,128)}, u32[]{:S(2)}, u32[]{:S(2)}) collective-permute-start(f32[768,768]{1,0:T(8,128)} %convolution_add_fusion.1), channel_id=1, source_target_pairs={{0,1},{1,0},{2,3},{3,2},{4,5},{5,4},{6,7},{7,6},{8,9},{9,8},{10,11... | collective-permute-start | bytes 7077896 | tf_op jit(solution)/shard_map/ppermute | solution.py:22
  176.9 28.2 %collective-permute-start.8 = (bf16[768,768]{1,0:T(8,128)(2,1)S(1)}, bf16[768,768]{1,0:T(8,128)(2,1)S(1)}, u32[]{:S(2)}, u32[]{:S(2)}) collective-permute-start(bf16[768,768]{1,0:T(8,128)(2,1)S(1)} %get-tuple-element.5), channel_id=1, source_target_pairs={{0,6},{1,7},{2,0},{3,1},{4,2},{5,3},{6,4},{7,5},{8,14},{9,15},{10,... | collective-permute-start | bytes 3538952 | tf_op jit(solution)/shard_map/ppermute | solution.py:16
  205.3 52.5 %collective-permute-start.9 = (bf16[768,768]{1,0:T(8,128)(2,1)S(1)}, bf16[768,768]{1,0:T(8,128)(2,1)S(1)}, u32[]{:S(2)}, u32[]{:S(2)}) collective-permute-start(bf16[768,768]{1,0:T(8,128)(2,1)S(1)} %broadcast_select_fusion.2), channel_id=1, source_target_pairs={{0,4},{1,5},{2,6},{3,7},{4,0},{5,1},{6,2},{7,3},{8,12},{9,13},{10,... | collective-permute-start | bytes 3538952 | tf_op jit(solution)/shard_map/ppermute | solution.py:16
  258.0 29.9 %copy-start.5 = (bf16[768,768]{1,0:T(8,128)(2,1)S(1)}, bf16[768,768]{1,0:T(8,128)(2,1)}, u32[]{:S(2)}) copy-start(bf16[768,768]{1,0:T(8,128)(2,1)} %copy-done.4) | copy-start | bytes 3538948
  258.0 28.8 %collective-permute-start.10 = (bf16[768,768]{1,0:T(8,128)(2,1)S(1)}, bf16[768,768]{1,0:T(8,128)(2,1)S(1)}, u32[]{:S(2)}, u32[]{:S(2)}) collective-permute-start(bf16[768,768]{1,0:T(8,128)(2,1)S(1)} %broadcast_select_fusion.4), channel_id=1, source_target_pairs={{0,6},{1,7},{2,0},{3,1},{4,2},{5,3},{6,4},{7,5},{8,14},{9,15},{10,... | collective-permute-start | bytes 3538952 | tf_op jit(solution)/shard_map/ppermute | solution.py:16
  288.9 4.0 %copy-start.1 = (pred[768,384]{1,0:T(8,128)(4,1)S(1)}, pred[768,384]{1,0:T(8,128)(4,1)}, u32[]{:S(2)}) copy-start(pred[768,384]{1,0:T(8,128)(4,1)} %copy-done) | copy-start | bytes 884740
  289.1 3.9 %collective-permute-start.11 = (f32[768,384]{1,0:T(8,128)S(1)}, f32[768,384]{1,0:T(8,128)S(1)}, u32[]{:S(2)}, u32[]{:S(2)}) collective-permute-start(f32[768,384]{1,0:T(8,128)S(1)} %slice_select_fusion.1), channel_id=1, source_target_pairs={{0,1},{1,0},{2,3},{3,2},{4,5},{5,4},{6,7},{7,6},{8,9},{9,8},{10,11... | collective-permute-start | bytes 3538952 | tf_op jit(solution)/shard_map/ppermute | solution.py:22
where the time goes:
time: 295 us; the launch traced here: 294 us
  waiting for transfers between devices  231 us (78%)
  starting transfers between devices  30.5 us (10%)
  blocking collectives  10.1 us (3%)
  other arithmetic  8.47 us (3%)
  local copies, waits for them, and re-layouts  8.18 us (3%)
  matrix products  5.8 us (2%)
    ppermute x9, waiting for transfers between devices, shifted_2(): lax.ppermute(array, axis, [(i, (i + by) % length) for i in range(length)])  204 us
    all_to_all x1, waiting for transfers between devices, per_device(): lax.all_to_all(lax.all_to_all(upper_stored, 'row', split_axis=1, concat_a...  15.8 us
    ppermute x9, starting transfers between devices, shifted_2(): lax.ppermute(array, axis, [(i, (i + by) % length) for i in range(length)])  14 us
    all_to_all x1, blocking collectives, per_device(): lax.all_to_all(upper_stored, 'row', split_axis=1, concat_axis=0, tiled=True)  10.1 us
    all_to_all x1, starting transfers between devices, per_device(): lax.all_to_all(lax.all_to_all(upper_stored, 'row', split_axis=1, concat_a...  6.67 us
  transfers between devices with their start and end apart: 14, of which 12 were waited for; matrix products, arithmetic and copies ran while one was open for 2% of the time, Pallas kernels for 0%

commit v1 on v0

--- a/solution.py
+++ b/solution.py
@@ -80,7 +80,7 @@
     return running
 
 
-def per_device(upper_stored, block_cells):
+def per_device_ring(upper_stored, block_cells):
     grid_size = lax.axis_size("row")
     row_id = lax.axis_index("row")
     col_id = lax.axis_index("col")
@@ -135,6 +135,46 @@
     return block_keep(3.0 * own_square - 2.0 * cubic, near_own).astype(jnp.bfloat16)
 
 
+def per_device_gather(upper_stored, block_cells):
+    row_id = lax.axis_index("row")
+    col_id = lax.axis_index("col")
+    rows, cols = upper_stored.shape
+    order_total = rows * lax.axis_size("row")
+    row_blocks, col_blocks = rows // BLK, cols // BLK
+    all_blocks = order_total // BLK
+    near_own = cell_mask(
+        block_cells, row_id * row_blocks, row_blocks, col_id * col_blocks, col_blocks, NEAR
+    )
+    global_rows = row_id * rows + lax.broadcasted_iota(jnp.int32, (rows, cols), 0)
+    global_cols = col_id * cols + lax.broadcasted_iota(jnp.int32, (rows, cols), 1)
+    diagonal = jnp.where(global_rows == global_cols, 0.5, 0.0).astype(jnp.float32)
+    value_scale = 2.0 / math.sqrt(order_total)
+    own_upper = block_keep(
+        diagonal + value_scale * upper_stored.astype(jnp.float32), near_own
+    ).astype(jnp.bfloat16)
+    blocks = lax.all_gather(own_upper, ("row", "col"))
+    grid = blocks.reshape(lax.axis_size("row"), lax.axis_size("col"), rows, cols)
+    upper = grid.transpose(0, 2, 1, 3).reshape(order_total, order_total)
+    i0 = lax.broadcasted_iota(jnp.int32, (order_total, order_total), 0)
+    i1 = lax.broadcasted_iota(jnp.int32, (order_total, order_total), 1)
+    density = jnp.where(i0 <= i1, upper, upper.T)
+    left = lax.dynamic_slice_in_dim(density, row_id * rows, rows, 0)
+    right = lax.dynamic_slice_in_dim(density, col_id * cols, cols, 1)
+    far = cell_mask(block_cells, row_id * row_blocks, row_blocks, 0, all_blocks, FAR)
+    square = block_keep(jnp.dot(left, density, preferred_element_type=jnp.float32), far)
+    square_low = square.astype(jnp.bfloat16)
+    own_square = lax.dynamic_slice_in_dim(square, col_id * cols, cols, 1)
+    cubic = jnp.dot(square_low, right, preferred_element_type=jnp.float32)
+    return block_keep(3.0 * own_square - 2.0 * cubic, near_own).astype(jnp.bfloat16)
+
+
+def per_device(upper_stored, block_cells):
+    order_total = upper_stored.shape[0] * lax.axis_size("row")
+    if order_total * order_total * 2 > 24 * 2**20:
+        return per_device_ring(upper_stored, block_cells)
+    return per_device_gather(upper_stored, block_cells)
+
+
 def solution(mesh):
     return jax.shard_map(
         per_device,

time: 295 us -> 240 us (0.81)
  waiting for transfers between devices: 231 us -> 109 us
  local copies, waits for them, and re-layouts: 8.18 us -> 68.7 us
  starting transfers between devices: 30.5 us -> 0.01 us
  matrix products: 5.8 us -> 25 us
  between operations: 0.23 us -> 13.5 us
  other arithmetic: 8.47 us -> 20.3 us
  blocking collectives: 10.1 us -> 0 us
    ppermute x12 -> x0, waiting for transfers between devices: 210 us -> none  [the longest x9 204 us: shifted_2(): lax.ppermute(array, axis, [(i, (i + by) % length) for i in range(length)])]
    all_gather x0 -> x1, waiting for transfers between devices: none -> 109 us  [per_device_gather(): blocks = lax.all_gather(own_upper, ('row', 'col'))]
    reshape x0 -> x2, local copies, waits for them, and re-layouts: none -> 41.2 us  [the longest x1 24.7 us: per_device_gather(): upper = grid.transpose(0, 2, 1, 3).reshape(order_total, order_total)]
    all_to_all x2 -> x0, waiting for transfers between devices: 21.1 us -> none  [the longest x1 15.8 us: per_device(): lax.all_to_all(lax.all_to_all(upper_stored, 'row', split_axis=1, concat_a...]
    dot_general x4 -> x2, matrix products: 5.8 us -> 25 us  [the longest x1 17.4 us: per_device_gather(): jnp.dot(left, density, preferred_element_type=jnp.float32)]
    ppermute x12 -> x0, starting transfers between devices: 18.5 us -> none  [the longest x9 14 us: shifted_2(): lax.ppermute(array, axis, [(i, (i + by) % length) for i in range(length)])]
    select_n x7 -> x1, other arithmetic: 3.65 us -> 17.2 us  [per_device_gather(): density = jnp.where(i0 <= i1, upper, upper.T)]
    broadcast_in_dim x4, local copies, waits for them, and re-layouts: 3.97 us -> 17.4 us  [block_keep(): jnp.where(keep_mask[:, None, :, None], shaped, jnp.zeros_like(shaped))]
  transfers between devices with their start and end apart: 14 -> 1, of which waited for: 12 -> 1; matrix products, arithmetic and copies ran while one was open for 2% -> 7% of each run, Pallas kernels for 0% -> 0%
where the time goes in v1:
time: 240 us; the launch traced here: 237 us
  waiting for transfers between devices  109 us (45%)
  local copies, waits for them, and re-layouts  68.7 us (29%)
  matrix products  25 us (10%)
  other arithmetic  20.3 us (8%)
  between operations  13.5 us (6%)
    all_gather x1, waiting for transfers between devices, per_device_gather(): blocks = lax.all_gather(own_upper, ('row', 'col'))  109 us
    reshape x1, local copies, waits for them, and re-layouts, per_device_gather(): upper = grid.transpose(0, 2, 1, 3).reshape(order_total, order_total)  24.7 us
    dot_general x1, matrix products, per_device_gather(): jnp.dot(left, density, preferred_element_type=jnp.float32)  17.4 us
    broadcast_in_dim x4, local copies, waits for them, and re-layouts, block_keep(): jnp.where(keep_mask[:, None, :, None], shaped, jnp.zeros_like(shaped))  17.4 us
    select_n x1, other arithmetic, per_device_gather(): density = jnp.where(i0 <= i1, upper, upper.T)  17.2 us
    reshape x1, local copies, waits for them, and re-layouts, per_device_gather(): blocks.reshape(lax.axis_size('row'), lax.axis_size('col'), rows, cols)  16.5 us
    unnamed x1, local copies, waits for them, and re-layouts  8.53 us
    dot_general x1, matrix products, per_device_gather(): cubic = jnp.dot(square_low, right, preferred_element_type=jnp.float32)  7.52 us
  transfers between devices with their start and end apart: 1, of which 1 were waited for; matrix products, arithmetic and copies ran while one was open for 7% of the time, Pallas kernels for 0%

profile of v1, /device:TPU:7, one launch (start us, length us, event | category | flops | bytes accessed | tf_op | source)
XLA Modules:
  0.0 236.5 jit_solution(9977216828631391508)
XLA Ops:
  6.5 0.0 all-gather.3.cloned.1.call-start
  6.5 0.8 constant_dynamic-slice_fusion.1
  7.3 0.8 constant_dynamic-slice_fusion
  8.0 0.1 fusion.28
  8.1 0.1 copy.14
  8.2 0.3 broadcast_in_dim.41
  8.5 1.4 broadcast_in_dim.42
  10.0 2.2 select_convert_fusion
  12.2 0.0 all-gather.3.cloned.1.call-update
  12.2 0.8 fusion.26
  13.0 3.4 %broadcast_in_dim.43 = pred[12,64,48,64]{3,2,1,0:T(8,128)(4,1)} broadcast(pred[12,48]{1,0:T(8,128)(4,1)S(1)} %broadcast_compare_fusion), dimensions={0,2} | broadcast | bytes 2359872 | tf_op jit(solution)/shard_map/jit(_where)/broadcast_in_dim | solution.py:39
  16.5 12.3 %broadcast_in_dim.44 = pred[768,3072]{1,0:T(32,128)(4,1)S(1)} reshape(pred[12,64,48,64]{3,2,1,0:T(8,128)(4,1)} %broadcast_in_dim.43) | data formatting | bytes 4718592 | tf_op jit(solution)/shard_map/jit(_where)/broadcast_in_dim | solution.py:39
  28.7 109.1 %all-gather.3.cloned.1.call-done = bf16[24576,384]{1,0:T(8,128)(2,1)} async-done(((bf16[768,384]{1,0:T(8,128)(2,1)}), bf16[24576,384]{1,0:T(8,128)(2,1)}) %all-gather.3.cloned.1.call-update) | async-done | bytes 18874384 | tf_op jit(solution)/shard_map/all_gather | solution.py:155
  137.8 16.5 %copy.15 = bf16[4,8,768,384]{3,1,2,0:T(8,128)(2,1)S(1)} copy(bf16[4,8,768,384]{3,2,1,0:T(8,128)(2,1)} %bitcast.13) | data formatting | bytes 37748736 | tf_op jit(solution)/shard_map/reshape | solution.py:156
  154.3 8.5 %copy.17 = bf16[384,8,8,384]{3,1,2,0:T(8,128)(2,1)} copy(bf16[384,8,8,384]{3,2,1,0:T(8,128)(2,1)S(1)} %bitcast.12) | data formatting | bytes 37748736
  162.9 24.7 %copy.16 = bf16[3072,3072]{0,1:T(8,128)(2,1)} copy(bf16[3072,3072]{1,0:T(8,128)(2,1)} %bitcast.10) | data formatting | bytes 37748736 | tf_op jit(solution)/shard_map/reshape | solution.py:157
  187.5 17.2 %fusion = bf16[3072,3072]{1,0:T(8,128)(2,1)S(1)} fusion(bf16[3072,3072]{1,0:T(8,128)(2,1)} %bitcast.11, bf16[3072,3072]{0,1:T(8,128)(2,1)} %copy.16), kind=kLoop, calls=%fused_computation.1 | loop fusion | flops 18874368 | bytes 56623104 | tf_op jit(solution)/shard_map/jit(_where)/select_n | solution.py:160
  204.7 17.4 %convolution_select_fusion = f32[768,3072]{1,0:T(8,128)} fusion(pred[768,3072]{1,0:T(32,128)(4,1)S(1)} %broadcast_in_dim.44, bf16[3072,3072]{1,0:T(8,128)(2,1)S(1)} %fusion, s32[]{:T(128)S(6)} %select_n.41), kind=kOutput, calls=%fused_computation.2 | convolution fusion | flops 14497873920 | bytes 35389444 | tf_op jit(solution)/shard_map/dot_general | solution.py:164
  222.2 7.5 %fusion.20 = bf16[768,384]{1,0:T(8,128)(2,1)} fusion(pred[768,384]{1,0:T(32,128)(4,1)S(1)} %broadcast_in_dim.42, bf16[3072,3072]{1,0:T(8,128)(2,1)S(1)} %fusion, s32[]{:T(128)S(6)} %select_n.43, f32[768,3072]{1,0:T(8,128)} %convolution_select_fusion), kind=kOutput, calls=%fused_computation.10 | convolution fusion | flops 1815773184 | bytes 13861888 | tf_op jit(solution)/shard_map/dot_general | solution.py:167
  (4 shorter events, 0.0 us)
Async XLA Ops:
  6.5 131.3 %all-gather.3.cloned.1.call-start = ((), (), s32[]{:S(2)}) async-start(), calls=%async_computation | async-start | bytes 19464192 | tf_op jit(solution)/shard_map/all_gather | solution.py:155
Sparse Core Ops, SparseCore 0:
  12.3 125.4 all-gather.2

commit v2 on v0

--- a/solution.py
+++ b/solution.py
@@ -3,6 +3,8 @@
 import jax
 import jax.numpy as jnp
 from jax import lax
+from jax.experimental import pallas as pl
+from jax.experimental.pallas import tpu as pltpu
 from jax.sharding import PartitionSpec as P
 
 BLK = 64
@@ -80,7 +82,7 @@
     return running
 
 
-def per_device(upper_stored, block_cells):
+def per_device_ring(upper_stored, block_cells):
     grid_size = lax.axis_size("row")
     row_id = lax.axis_index("row")
     col_id = lax.axis_index("col")
@@ -135,6 +137,128 @@
     return block_keep(3.0 * own_square - 2.0 * cubic, near_own).astype(jnp.bfloat16)
 
 
+def wrapped_square(row_cells, col_cells):
+    total = 0
+    for axis in range(3):
+        offset = jnp.abs(row_cells[axis] - col_cells[axis])
+        wrapped = jnp.minimum(offset, BOX - offset)
+        total = total + wrapped * wrapped
+    return total
+
+
+def masked_density(upper_stored, block_cells):
+    rows, cols = upper_stored.shape
+    row_start = lax.axis_index("row") * rows
+    col_start = lax.axis_index("col") * cols
+    order_total = rows * lax.axis_size("row")
+    row_cells = lax.dynamic_slice_in_dim(block_cells, row_start // BLK, rows // BLK, 0)
+    col_cells = lax.dynamic_slice_in_dim(block_cells, col_start // BLK, cols // BLK, 0)
+    row_cells = jnp.repeat(row_cells, BLK, axis=0)
+    col_cells = jnp.repeat(col_cells, BLK, axis=0)
+    near = wrapped_square(
+        [row_cells[:, a][:, None] for a in range(3)], [col_cells[:, a][None, :] for a in range(3)]
+    )
+    global_rows = row_start + lax.broadcasted_iota(jnp.int32, (rows, cols), 0)
+    global_cols = col_start + lax.broadcasted_iota(jnp.int32, (rows, cols), 1)
+    diagonal = jnp.where(global_rows == global_cols, 0.5, 0.0).astype(jnp.float32)
+    value = diagonal + (2.0 / math.sqrt(order_total)) * upper_stored.astype(jnp.float32)
+    return jnp.where(near <= NEAR, value, 0.0).astype(jnp.bfloat16)
+
+
+def purify_kernel(cells_ref, lanes_ref, blocks_ref, out_ref, density, square_low, own, sems):
+    rows, cols = out_ref.shape
+    order_total = density.shape[0]
+    columns = order_total // cols
+    per_row = rows // cols
+    row_id = lax.axis_index("row")
+    col_id = lax.axis_index("col")
+
+    def load(i, j):
+        return pltpu.make_async_copy(
+            blocks_ref.at[(i // per_row) * columns + j, pl.ds((i % per_row) * cols, cols)],
+            density.at[pl.ds(i * cols, cols), pl.ds(j * cols, cols)],
+            sems.at[i * columns + j],
+        )
+
+    pairs = [(i, j) for j in range(columns) for i in range(j + 1)]
+    for i, j in pairs:
+        load(i, j).start()
+    below = lax.broadcasted_iota(jnp.int32, (cols, cols), 0) > lax.broadcasted_iota(
+        jnp.int32, (cols, cols), 1
+    )
+    for i, j in pairs:
+        load(i, j).wait()
+        upper = density[i * cols : (i + 1) * cols, j * cols : (j + 1) * cols]
+        flipped = upper.T
+        if i == j:
+            flipped = jnp.where(below, flipped, upper)
+        density[j * cols : (j + 1) * cols, i * cols : (i + 1) * cols] = flipped
+
+    def keep(value, lanes, bound):
+        pieces = []
+        for block in range(rows // BLK):
+            row = row_id * (rows // BLK) + block
+            distance = wrapped_square(
+                [cells_ref[row, a] for a in range(3)], [lanes[a : a + 1, :] for a in range(3)]
+            )
+            piece = value[block * BLK : (block + 1) * BLK]
+            pieces.append(jnp.where(distance <= bound, piece, 0.0))
+        return jnp.concatenate(pieces, 0)
+
+    own_rows = pl.ds(pl.multiple_of(row_id * rows, rows), rows)
+
+    @pl.loop(0, columns)
+    def _(j):
+        here = pl.ds(pl.multiple_of(j * cols, cols), cols)
+        product = jnp.dot(
+            density[own_rows, :], density[:, here], preferred_element_type=jnp.float32
+        )
+        square = keep(product, lanes_ref[:, here], FAR)
+        square_low[:, here] = square.astype(jnp.bfloat16)
+
+        @pl.when(j == col_id)
+        def _():
+            own[...] = square
+
+    mine = pl.ds(pl.multiple_of(col_id * cols, cols), cols)
+    cubic = jnp.dot(square_low[...], density[:, mine], preferred_element_type=jnp.float32)
+    result = 3.0 * own[...] - 2.0 * cubic
+    out_ref[...] = keep(result, lanes_ref[:, mine], NEAR).astype(jnp.bfloat16)
+
+
+def per_device_gather(upper_stored, block_cells):
+    rows, cols = upper_stored.shape
+    order_total = rows * lax.axis_size("row")
+    columns = order_total // cols
+    blocks = lax.all_gather(masked_density(upper_stored, block_cells), ("row", "col"))
+    lanes = jnp.zeros((8, order_total), jnp.int32).at[:3].set(jnp.repeat(block_cells, BLK, axis=0).T)
+    vmem = pl.BlockSpec(memory_space=pltpu.VMEM)
+    return pl.pallas_call(
+        purify_kernel,
+        out_shape=jax.ShapeDtypeStruct((rows, cols), jnp.bfloat16),
+        in_specs=[
+            pl.BlockSpec(memory_space=pltpu.SMEM),
+            vmem,
+            pl.BlockSpec(memory_space=pl.ANY),
+        ],
+        out_specs=vmem,
+        scratch_shapes=[
+            pltpu.VMEM((order_total, order_total), jnp.bfloat16),
+            pltpu.VMEM((rows, order_total), jnp.bfloat16),
+            pltpu.VMEM((rows, cols), jnp.float32),
+            pltpu.SemaphoreType.DMA((columns * columns,)),
+        ],
+        compiler_params=pltpu.CompilerParams(vmem_limit_bytes=48 * 2**20),
+    )(block_cells, lanes, blocks)
+
+
+def per_device(upper_stored, block_cells):
+    order_total = upper_stored.shape[0] * lax.axis_size("row")
+    if order_total * order_total * 2 > 24 * 2**20:
+        return per_device_ring(upper_stored, block_cells)
+    return per_device_gather(upper_stored, block_cells)
+
+
 def solution(mesh):
     return jax.shard_map(
         per_device,

time: 295 us -> 179 us (0.61)
  waiting for transfers between devices: 231 us -> 125 us
  Pallas kernels: 0 us -> 32.2 us
  starting transfers between devices: 30.5 us -> 0.01 us
  between operations: 0.23 us -> 13.5 us
  blocking collectives: 10.1 us -> 0 us
  local copies, waits for them, and re-layouts: 8.18 us -> 2.22 us
  matrix products: 5.8 us -> 0 us
  other arithmetic: 8.47 us -> 3.64 us
    ppermute x12 -> x0, waiting for transfers between devices: 210 us -> none  [the longest x9 204 us: shifted_2(): lax.ppermute(array, axis, [(i, (i + by) % length) for i in range(length)])]
    all_gather x0 -> x1, waiting for transfers between devices: none -> 125 us  [per_device_gather(): lax.all_gather(masked_density(upper_stored, block_cells), ('row', 'col'))]
    pallas_call x0 -> x1, Pallas kernels: none -> 32.2 us  [per_device_gather(): pl.pallas_call(purify_kernel, out_shape=jax.ShapeDtypeStruct((rows, cols)...]
    all_to_all x2 -> x0, waiting for transfers between devices: 21.1 us -> none  [the longest x1 15.8 us: per_device(): lax.all_to_all(lax.all_to_all(upper_stored, 'row', split_axis=1, concat_a...]
    ppermute x12 -> x0, starting transfers between devices: 18.5 us -> none  [the longest x9 14 us: shifted_2(): lax.ppermute(array, axis, [(i, (i + by) % length) for i in range(length)])]
    all_to_all x2 -> x0, starting transfers between devices: 12 us -> none  [the longest x1 6.67 us: per_device(): lax.all_to_all(lax.all_to_all(upper_stored, 'row', split_axis=1, concat_a...]
    all_to_all x1 -> x0, blocking collectives: 10.1 us -> none  [per_device(): lax.all_to_all(upper_stored, 'row', split_axis=1, concat_axis=0, tiled=True)]
    dot_general x4 -> x0, matrix products: 5.8 us -> none  [cannon_half(): running = running + jnp.dot(left, right, preferred_element_type=jnp.float32)]
  transfers between devices with their start and end apart: 14 -> 1, of which waited for: 12 -> 1; matrix products, arithmetic and copies ran while one was open for 2% -> 0% of each run, Pallas kernels for 0% -> 0%
where the time goes in v2:
time: 179 us; the launch traced here: 177 us
  waiting for transfers between devices  125 us (70%)
  Pallas kernels  32.2 us (18%)
  between operations  13.5 us (8%)
  other arithmetic  3.64 us (2%)
  local copies, waits for them, and re-layouts  2.22 us (1%)
    all_gather x1, waiting for transfers between devices, per_device_gather(): lax.all_gather(masked_density(upper_stored, block_cells), ('row', 'col'))  125 us
    pallas_call x1, Pallas kernels, per_device_gather(): pl.pallas_call(purify_kernel, out_shape=jax.ShapeDtypeStruct((rows, cols)...  32.2 us
    convert_element_type x1, other arithmetic, masked_density(): return jnp.where(near <= NEAR, value, 0.0).astype(jnp.bfloat16)  3.64 us
  transfers between devices with their start and end apart: 1, of which 1 were waited for; matrix products, arithmetic and copies ran while one was open for 0% of the time, Pallas kernels for 0%

profile of v2, /device:TPU:7, one launch (start us, length us, event | category | flops | bytes accessed | tf_op | source)
XLA Modules:
  0.0 176.8 jit_solution(7436227398846008669)
XLA Ops:
  6.5 0.0 copy-start
  6.5 0.0 all-gather.3.cloned.1.call-start
  6.6 0.8 constant_dynamic-slice_fusion.1
  7.4 0.1 broadcast_in_dim.21
  7.4 0.1 reshape.39
  7.6 0.8 constant_dynamic-slice_fusion
  8.3 0.1 broadcast_in_dim.22
  8.4 0.1 reshape.40
  8.5 3.6 %select_convert_fusion = bf16[768,384]{1,0:T(8,128)(2,1)} fusion(bf16[768,384]{1,0:T(8,128)(2,1)} %param.4, s32[384]{0:T(512)S(1)} %iota_add_fusion.1, s32[384]{0:T(512)S(1)} %get-tuple-element.21, s32[768]{0:T(1024)S(1)} %get-tuple-element.18, s32[384]{0:T(512)S(1)} %get-tuple-element.22, s32[768]{0:T(1024)S(1)} %get-tuple-element.19, ...), kind=kLoop, calls=%fused_computation.9 | loop fusion | flops 7372800 | bytes 1198080 | tf_op jit(solution)/shard_map/convert_element_type | solution.py:165
  12.1 0.0 all-gather.3.cloned.1.call-update
  12.2 0.0 copy-done
  12.2 0.1 copy.6.cells_ref
  12.3 0.1 broadcast_in_dim.20
  12.3 0.1 reshape.38
  12.5 125.3 %all-gather.3.cloned.1.call-done = bf16[24576,384]{1,0:T(8,128)(2,1)} async-done(((bf16[768,384]{1,0:T(8,128)(2,1)}), bf16[24576,384]{1,0:T(8,128)(2,1)}) %all-gather.3.cloned.1.call-update) | async-done | bytes 18874384 | tf_op jit(solution)/shard_map/all_gather | solution.py:233
  137.8 32.2 %shard_map.28 = bf16[768,384]{1,0:T(8,128)(2,1)} custom-call(s32[48,3]{1,0:T(8,128)S(1)} %copy.6.cells_ref, s32[8,3072]{1,0:T(8,128)S(1)} %scatter.4.lanes_ref, bf16[32,768,384]{2,1,0:T(8,128)(2,1)} %bitcast.8), custom_call_target="tpu_custom_call" | custom-call | tf_op jit(solution)/shard_map/pallas_call | solution.py:236
  (5 shorter events, 0.1 us)
Async XLA Ops:
  6.5 5.6 %copy-start = (s32[48,3]{0,1:T(4,128)S(1)}, s32[48,3]{0,1:T(4,128)}, u32[]{:S(2)}) copy-start(s32[48,3]{0,1:T(4,128)} %param.5) | copy-start | bytes 1732
  6.5 131.2 %all-gather.3.cloned.1.call-start = ((), (), s32[]{:S(2)}) async-start(), calls=%async_computation | async-start | bytes 19464192 | tf_op jit(solution)/shard_map/all_gather | solution.py:233
Sparse Core Ops, SparseCore 0:
  12.3 125.4 all-gather.2

commit v3 on v2

--- a/solution.py
+++ b/solution.py
@@ -226,11 +226,198 @@
     out_ref[...] = keep(result, lanes_ref[:, mine], NEAR).astype(jnp.bfloat16)
 
 
+def gather_kernel(
+    own_ref, blocks_ref, z_send, z_recv, p_send, p_recv, d_send, d_recv, c_send, c_recv, local_sem
+):
+    rows = own_ref.shape[0]
+    half = rows // 2
+    columns = lax.axis_size("col")
+    layers = columns // 2
+    row_id = lax.axis_index("row")
+    col_id = lax.axis_index("col")
+    z, core = col_id // 2, col_id % 2
+    x_row = row_id + 1 - 2 * (row_id % 2)
+    y_row = (row_id + 2) % 4
+    diag_row = (x_row + 2) % 4
+    mesh_id = pl.DeviceIdType.MESH
+    to_x, to_y = (x_row, col_id), (y_row, col_id)
+    to_core = (row_id, col_id + 1 - 2 * core)
+    up, down = (row_id, col_id + 2), (row_id, col_id - 2)
+    has_up, has_down = z + 1 < layers, z > 0
+
+    barrier = pltpu.get_barrier_semaphore()
+    for target in (to_x, to_y, to_core):
+        pl.semaphore_signal(barrier, inc=1, device_id=target, device_id_type=mesh_id)
+
+    @pl.when(has_up)
+    def _():
+        pl.semaphore_signal(barrier, inc=1, device_id=up, device_id_type=mesh_id)
+
+    @pl.when(has_down)
+    def _():
+        pl.semaphore_signal(barrier, inc=1, device_id=down, device_id_type=mesh_id)
+
+    pl.semaphore_wait(barrier, 3 + has_up.astype(jnp.int32) + has_down.astype(jnp.int32))
+
+    far_slot = layers - 1
+    slots = [0]
+    for step in range(far_slot):
+        slots += [1 + step, 1 + far_slot + step]
+
+    def layer(slot):
+        if slot == 0:
+            return z
+        if slot <= far_slot:
+            return z - slot
+        return z + slot - far_slot
+
+    def valid(slot, act):
+        if slot == 0:
+            act()
+        elif slot <= far_slot:
+            pl.when(z >= slot)(act)
+        else:
+            pl.when(z + slot - far_slot < layers)(act)
+
+    def part(row, slot, piece):
+        index = row * columns + 2 * layer(slot) + core
+        block = blocks_ref.at[index]
+        return block if piece is None else block.at[pl.ds(piece * half, half)]
+
+    def copy(row, slot, piece, target, send, recv, first=False):
+        place = part(row, slot, piece)
+        return pltpu.make_async_remote_copy(
+            src_ref=own_ref if first else place,
+            dst_ref=place,
+            send_sem=send,
+            recv_sem=recv,
+            device_id=target,
+            device_id_type=mesh_id,
+        )
+
+    def z_up(slot):
+        return copy(row_id, slot, None, up, z_send.at[slot, 0], z_recv.at[slot + 1], slot == 0)
+
+    def z_down(slot):
+        later = 1 + far_slot if slot == 0 else slot + 1
+        return copy(row_id, slot, None, down, z_send.at[slot, 1], z_recv.at[later], slot == 0)
+
+    def goes_up(slot):
+        return slot < far_slot
+
+    def goes_down(slot):
+        return slot == 0 or far_slot < slot < 2 * far_slot
+
+    def plane(slot, way):
+        return copy(
+            row_id, slot, None, (to_x, to_y)[way], p_send.at[slot, way], p_recv.at[slot, way], slot == 0
+        )
+
+    def relay(slot, way):
+        row = (x_row, y_row)[way]
+        target = (to_y, to_x)[way]
+        return copy(row, slot, way, target, d_send.at[slot, way], d_recv.at[slot, way])
+
+    def across(slot, kind):
+        row = (row_id, x_row, y_row, diag_row, diag_row)[kind]
+        piece = (None, None, None, 0, 1)[kind]
+        return copy(
+            row, slot, piece, to_core, c_send.at[slot, kind], c_recv.at[slot, kind],
+            slot == 0 and kind == 0,
+        )
+
+    def stage_own(slot):
+        def act():
+            if slot:
+                copy(row_id, slot, None, up, z_send.at[slot, 0], z_recv.at[slot]).wait_recv()
+            if goes_up(slot):
+                pl.when(has_up)(lambda: z_up(slot).start())
+            if goes_down(slot):
+                pl.when(has_down)(lambda: z_down(slot).start())
+            plane(slot, 0).start()
+            plane(slot, 1).start()
+            across(slot, 0).start()
+
+        valid(slot, act)
+
+    def stage_relay(slot):
+        def act():
+            for way in range(2):
+                plane_in = (x_row, y_row)[way]
+                copy(
+                    plane_in, slot, None, to_x, p_send.at[slot, way], p_recv.at[slot, way]
+                ).wait_recv()
+                relay(slot, way).start()
+                across(slot, 1 + way).start()
+
+        valid(slot, act)
+
+    def stage_diag(slot):
+        def act():
+            for way in range(2):
+                copy(
+                    diag_row, slot, way, to_x, d_send.at[slot, way], d_recv.at[slot, way]
+                ).wait_recv()
+                across(slot, 3 + way).start()
+
+        valid(slot, act)
+
+    def stage_end(slot):
+        def act():
+            if goes_up(slot):
+                pl.when(has_up)(lambda: z_up(slot).wait_send())
+            if goes_down(slot):
+                pl.when(has_down)(lambda: z_down(slot).wait_send())
+            for way in range(2):
+                plane(slot, way).wait_send()
+                relay(slot, way).wait_send()
+            for kind in range(5):
+                across(slot, kind).wait()
+
+        valid(slot, act)
+
+    keep_own = pltpu.make_async_copy(own_ref, part(row_id, 0, None), local_sem)
+    keep_own.start()
+    for turn in range(len(slots) + 2):
+        if turn < len(slots):
+            stage_own(slots[turn])
+        if 1 <= turn <= len(slots):
+            stage_relay(slots[turn - 1])
+        if turn >= 2:
+            stage_diag(slots[turn - 2])
+    for slot in slots:
+        stage_end(slot)
+    keep_own.wait()
+
+
+def gather_blocks(own):
+    rows, cols = own.shape
+    columns = lax.axis_size("col")
+    count = lax.axis_size("row") * columns
+    slots = columns - 1
+    dma = pltpu.SemaphoreType.DMA
+    anywhere = pl.BlockSpec(memory_space=pl.ANY)
+    return pl.pallas_call(
+        gather_kernel,
+        out_shape=jax.ShapeDtypeStruct((count, rows, cols), own.dtype),
+        in_specs=[anywhere],
+        out_specs=anywhere,
+        scratch_shapes=[
+            dma((slots, 2)), dma((slots,)),
+            dma((slots, 2)), dma((slots, 2)),
+            dma((slots, 2)), dma((slots, 2)),
+            dma((slots, 5)), dma((slots, 5)),
+            dma,
+        ],
+        compiler_params=pltpu.CompilerParams(collective_id=0, has_side_effects=True),
+    )(own)
+
+
 def per_device_gather(upper_stored, block_cells):
     rows, cols = upper_stored.shape
     order_total = rows * lax.axis_size("row")
     columns = order_total // cols
-    blocks = lax.all_gather(masked_density(upper_stored, block_cells), ("row", "col"))
+    blocks = gather_blocks(masked_density(upper_stored, block_cells))
     lanes = jnp.zeros((8, order_total), jnp.int32).at[:3].set(jnp.repeat(block_cells, BLK, axis=0).T)
     vmem = pl.BlockSpec(memory_space=pltpu.VMEM)
     return pl.pallas_call(
@@ -254,7 +441,7 @@
 
 def per_device(upper_stored, block_cells):
     order_total = upper_stored.shape[0] * lax.axis_size("row")
-    if order_total * order_total * 2 > 24 * 2**20:
+    if lax.axis_size("row") != 4 or order_total * order_total * 2 > 24 * 2**20:
         return per_device_ring(upper_stored, block_cells)
     return per_device_gather(upper_stored, block_cells)
 

time: 179 us -> 132 us (0.74)
  waiting for transfers between devices: 125 us -> 0 us
  Pallas kernels: 32.2 us -> 123 us
  between operations: 13.5 us -> 0.04 us
    all_gather x1 -> x0, waiting for transfers between devices: 125 us -> none  [per_device_gather(): lax.all_gather(masked_density(upper_stored, block_cells), ('row', 'col'))]
    pallas_call x0 -> x1, Pallas kernels: none -> 90.3 us  [gather_blocks(): pl.pallas_call(gather_kernel, out_shape=jax.ShapeDtypeStruct((count, rows...]
  transfers between devices with their start and end apart: 1 -> 0, of which waited for: 1 -> 0; matrix products, arithmetic and copies ran while one was open for 0% -> 0% of each run, Pallas kernels for 0% -> 0%
where the time goes in v3:
time: 132 us; the launch traced here: 130 us
  Pallas kernels  123 us (93%)
  other arithmetic  3.65 us (3%)
  local copies, waits for them, and re-layouts  3.5 us (3%)
    pallas_call x1, Pallas kernels, gather_blocks(): pl.pallas_call(gather_kernel, out_shape=jax.ShapeDtypeStruct((count, rows...  90.3 us
    pallas_call x1, Pallas kernels, per_device_gather(): pl.pallas_call(purify_kernel, out_shape=jax.ShapeDtypeStruct((rows, cols)...  32.2 us
    convert_element_type x1, other arithmetic, masked_density(): return jnp.where(near <= NEAR, value, 0.0).astype(jnp.bfloat16)  3.64 us

profile of v3, /device:TPU:7, one launch (start us, length us, event | category | flops | bytes accessed | tf_op | source)
XLA Modules:
  0.0 129.7 jit_solution(18250765011583349109)
XLA Ops:
  0.0 0.8 constant_dynamic-slice_fusion.1
  0.8 0.8 constant_dynamic-slice_fusion
  1.5 0.1 broadcast_in_dim.22
  1.6 0.1 reshape.40
  1.7 0.1 broadcast_in_dim.21
  1.8 0.1 reshape.39
  1.9 0.8 copy.6.cells_ref
  2.7 0.8 broadcast_in_dim.20
  3.4 0.1 reshape.38
  3.5 3.6 %select_convert_fusion.own_ref = bf16[768,384]{1,0:T(8,128)(2,1)} fusion(bf16[768,384]{1,0:T(8,128)(2,1)} %param.4, s32[384]{0:T(512)S(1)} %iota_add_fusion.1, s32[384]{0:T(512)S(1)} %get-tuple-element.21, s32[768]{0:T(1024)S(1)} %get-tuple-element.18, s32[384]{0:T(512)S(1)} %get-tuple-element.22, s32[768]{0:T(1024)S(1)} %get-tuple-element.19, ...), kind=kLoop, calls=%fused_computation.9 | loop fusion | flops 7372800 | bytes 1198080 | tf_op jit(solution)/shard_map/convert_element_type | solution.py:165
  7.2 90.3 %shard_map.28.blocks_ref = bf16[32,768,384]{2,1,0:T(8,128)(2,1)} custom-call(bf16[768,384]{1,0:T(8,128)(2,1)} %select_convert_fusion.own_ref), custom_call_target="tpu_custom_call" | custom-call | tf_op jit(solution)/shard_map/pallas_call | solution.py:400
  97.5 32.2 %shard_map.29 = bf16[768,384]{1,0:T(8,128)(2,1)} custom-call(s32[48,3]{1,0:T(8,128)S(1)} %copy.6.cells_ref, s32[8,3072]{1,0:T(8,128)S(1)} %scatter.4.lanes_ref, bf16[32,768,384]{2,1,0:T(8,128)(2,1)} %shard_map.28.blocks_ref), custom_call_target="tpu_custom_call" | custom-call | tf_op jit(solution)/shard_map/pallas_call | solution.py:423
  (5 shorter events, 0.1 us)

commit v4 on v3

--- a/solution.py
+++ b/solution.py
@@ -279,6 +279,9 @@
         else:
             pl.when(z + slot - far_slot < layers)(act)
 
+    def used(row, slot, act):
+        pl.when(row * rows < (2 * layer(slot) + 2) * own_ref.shape[1])(act)
+
     def part(row, slot, piece):
         index = row * columns + 2 * layer(slot) + core
         block = blocks_ref.at[index]
@@ -338,17 +341,20 @@
             plane(slot, 1).start()
             across(slot, 0).start()
 
-        valid(slot, act)
+        valid(slot, lambda: used(row_id, slot, act))
 
     def stage_relay(slot):
+        def one(way):
+            plane_in = (x_row, y_row)[way]
+            copy(
+                plane_in, slot, None, to_x, p_send.at[slot, way], p_recv.at[slot, way]
+            ).wait_recv()
+            relay(slot, way).start()
+            across(slot, 1 + way).start()
+
         def act():
-            for way in range(2):
-                plane_in = (x_row, y_row)[way]
-                copy(
-                    plane_in, slot, None, to_x, p_send.at[slot, way], p_recv.at[slot, way]
-                ).wait_recv()
-                relay(slot, way).start()
-                across(slot, 1 + way).start()
+            used(x_row, slot, lambda: one(0))
+            used(y_row, slot, lambda: one(1))
 
         valid(slot, act)
 
@@ -360,19 +366,31 @@
                 ).wait_recv()
                 across(slot, 3 + way).start()
 
-        valid(slot, act)
+        valid(slot, lambda: used(diag_row, slot, act))
 
     def stage_end(slot):
-        def act():
+        def own_end():
             if goes_up(slot):
                 pl.when(has_up)(lambda: z_up(slot).wait_send())
             if goes_down(slot):
                 pl.when(has_down)(lambda: z_down(slot).wait_send())
             for way in range(2):
                 plane(slot, way).wait_send()
-                relay(slot, way).wait_send()
-            for kind in range(5):
-                across(slot, kind).wait()
+            across(slot, 0).wait()
+
+        def relay_end(way):
+            relay(slot, way).wait_send()
+            across(slot, 1 + way).wait()
+
+        def diag_end():
+            across(slot, 3).wait()
+            across(slot, 4).wait()
+
+        def act():
+            used(row_id, slot, own_end)
+            used(x_row, slot, lambda: relay_end(0))
+            used(y_row, slot, lambda: relay_end(1))
+            used(diag_row, slot, diag_end)
 
         valid(slot, act)
 

time: 132 us -> 125 us (0.947)
  Pallas kernels: 123 us -> 115 us
    pallas_call x1, Pallas kernels: 90.3 us -> 83.2 us  [gather_blocks(): pl.pallas_call(gather_kernel, out_shape=jax.ShapeDtypeStruct((count, rows...]
where the time goes in v4:
time: 125 us; the launch traced here: 123 us
  Pallas kernels  115 us (92%)
  other arithmetic  3.65 us (3%)
  local copies, waits for them, and re-layouts  3.5 us (3%)
    pallas_call x1, Pallas kernels, gather_blocks(): pl.pallas_call(gather_kernel, out_shape=jax.ShapeDtypeStruct((count, rows...  83.2 us
    pallas_call x1, Pallas kernels, per_device_gather(): pl.pallas_call(purify_kernel, out_shape=jax.ShapeDtypeStruct((rows, cols)...  32.2 us
    convert_element_type x1, other arithmetic, masked_density(): return jnp.where(near <= NEAR, value, 0.0).astype(jnp.bfloat16)  3.64 us

profile of v4, /device:TPU:7, one launch (start us, length us, event | category | flops | bytes accessed | tf_op | source)
XLA Modules:
  0.0 122.6 jit_solution(7639526105849563489)
XLA Ops:
  0.0 0.8 constant_dynamic-slice_fusion.1
  0.8 0.8 constant_dynamic-slice_fusion
  1.5 0.1 broadcast_in_dim.22
  1.6 0.1 reshape.40
  1.7 0.1 broadcast_in_dim.21
  1.8 0.1 reshape.39
  1.9 0.8 copy.6.cells_ref
  2.7 0.8 broadcast_in_dim.20
  3.4 0.1 reshape.38
  3.5 3.6 %select_convert_fusion.own_ref = bf16[768,384]{1,0:T(8,128)(2,1)} fusion(bf16[768,384]{1,0:T(8,128)(2,1)} %param.4, s32[384]{0:T(512)S(1)} %iota_add_fusion.1, s32[384]{0:T(512)S(1)} %get-tuple-element.21, s32[768]{0:T(1024)S(1)} %get-tuple-element.18, s32[384]{0:T(512)S(1)} %get-tuple-element.22, s32[768]{0:T(1024)S(1)} %get-tuple-element.19, ...), kind=kLoop, calls=%fused_computation.9 | loop fusion | flops 7372800 | bytes 1198080 | tf_op jit(solution)/shard_map/convert_element_type | solution.py:165
  7.2 83.2 %shard_map.28.blocks_ref = bf16[32,768,384]{2,1,0:T(8,128)(2,1)} custom-call(bf16[768,384]{1,0:T(8,128)(2,1)} %select_convert_fusion.own_ref), custom_call_target="tpu_custom_call" | custom-call | tf_op jit(solution)/shard_map/pallas_call | solution.py:418
  90.4 32.2 %shard_map.29 = bf16[768,384]{1,0:T(8,128)(2,1)} custom-call(s32[48,3]{1,0:T(8,128)S(1)} %copy.6.cells_ref, s32[8,3072]{1,0:T(8,128)S(1)} %scatter.4.lanes_ref, bf16[32,768,384]{2,1,0:T(8,128)(2,1)} %shard_map.28.blocks_ref), custom_call_target="tpu_custom_call" | custom-call | tf_op jit(solution)/shard_map/pallas_call | solution.py:441
  (5 shorter events, 0.1 us)

commit v5 on v4

--- a/solution.py
+++ b/solution.py
@@ -230,7 +230,7 @@
     own_ref, blocks_ref, z_send, z_recv, p_send, p_recv, d_send, d_recv, c_send, c_recv, local_sem
 ):
     rows = own_ref.shape[0]
-    half = rows // 2
+    cut = rows * 3 // 8 // 16 * 16
     columns = lax.axis_size("col")
     layers = columns // 2
     row_id = lax.axis_index("row")
@@ -285,7 +285,9 @@
     def part(row, slot, piece):
         index = row * columns + 2 * layer(slot) + core
         block = blocks_ref.at[index]
-        return block if piece is None else block.at[pl.ds(piece * half, half)]
+        if piece is None:
+            return block
+        return block.at[pl.ds(0, cut) if piece == 0 else pl.ds(cut, rows - cut)]
 
     def copy(row, slot, piece, target, send, recv, first=False):
         place = part(row, slot, piece)
@@ -316,10 +318,18 @@
             row_id, slot, None, (to_x, to_y)[way], p_send.at[slot, way], p_recv.at[slot, way], slot == 0
         )
 
-    def relay(slot, way):
+    def relay(slot, way, piece):
         row = (x_row, y_row)[way]
         target = (to_y, to_x)[way]
-        return copy(row, slot, way, target, d_send.at[slot, way], d_recv.at[slot, way])
+        return copy(
+            row, slot, piece, target, d_send.at[slot, 2 * way + piece], d_recv.at[slot, piece]
+        )
+
+    def each_relay(slot, way, act):
+        row = (x_row, y_row)[way]
+        first = (row != 1, row == 2) if way == 0 else (row == 1, row != 2)
+        for piece in range(2):
+            pl.when(first[piece])(lambda piece=piece: act(relay(slot, way, piece)))
 
     def across(slot, kind):
         row = (row_id, x_row, y_row, diag_row, diag_row)[kind]
@@ -349,7 +359,7 @@
             copy(
                 plane_in, slot, None, to_x, p_send.at[slot, way], p_recv.at[slot, way]
             ).wait_recv()
-            relay(slot, way).start()
+            each_relay(slot, way, lambda c: c.start())
             across(slot, 1 + way).start()
 
         def act():
@@ -379,7 +389,7 @@
             across(slot, 0).wait()
 
         def relay_end(way):
-            relay(slot, way).wait_send()
+            each_relay(slot, way, lambda c: c.wait_send())
             across(slot, 1 + way).wait()
 
         def diag_end():
@@ -423,7 +433,7 @@
         scratch_shapes=[
             dma((slots, 2)), dma((slots,)),
             dma((slots, 2)), dma((slots, 2)),
-            dma((slots, 2)), dma((slots, 2)),
+            dma((slots, 4)), dma((slots, 2)),
             dma((slots, 5)), dma((slots, 5)),
             dma,
         ],

time: 125 us -> 133 us (1.064)
  Pallas kernels: 115 us -> 124 us
    pallas_call x1, Pallas kernels: 83.2 us -> 91.5 us  [gather_blocks(): pl.pallas_call(gather_kernel, out_shape=jax.ShapeDtypeStruct((count, rows...]
where the time goes in v5:
time: 133 us; the launch traced here: 131 us
  Pallas kernels  124 us (93%)
  other arithmetic  3.65 us (3%)
  local copies, waits for them, and re-layouts  3.5 us (3%)
    pallas_call x1, Pallas kernels, gather_blocks(): pl.pallas_call(gather_kernel, out_shape=jax.ShapeDtypeStruct((count, rows...  91.5 us
    pallas_call x1, Pallas kernels, per_device_gather(): pl.pallas_call(purify_kernel, out_shape=jax.ShapeDtypeStruct((rows, cols)...  32.2 us
    convert_element_type x1, other arithmetic, masked_density(): return jnp.where(near <= NEAR, value, 0.0).astype(jnp.bfloat16)  3.64 us

profile of v5, /device:TPU:7, one launch (start us, length us, event | category | flops | bytes accessed | tf_op | source)
XLA Modules:
  0.0 130.9 jit_solution(9593236901648721522)
XLA Ops:
  0.0 0.8 constant_dynamic-slice_fusion.1
  0.8 0.8 constant_dynamic-slice_fusion
  1.5 0.1 broadcast_in_dim.22
  1.6 0.1 reshape.40
  1.7 0.1 broadcast_in_dim.21
  1.8 0.1 reshape.39
  1.9 0.8 copy.6.cells_ref
  2.7 0.8 broadcast_in_dim.20
  3.4 0.1 reshape.38
  3.5 3.6 %select_convert_fusion.own_ref = bf16[768,384]{1,0:T(8,128)(2,1)} fusion(bf16[768,384]{1,0:T(8,128)(2,1)} %param.4, s32[384]{0:T(512)S(1)} %iota_add_fusion.1, s32[384]{0:T(512)S(1)} %get-tuple-element.21, s32[768]{0:T(1024)S(1)} %get-tuple-element.18, s32[384]{0:T(512)S(1)} %get-tuple-element.22, s32[768]{0:T(1024)S(1)} %get-tuple-element.19, ...), kind=kLoop, calls=%fused_computation.9 | loop fusion | flops 7372800 | bytes 1198080 | tf_op jit(solution)/shard_map/convert_element_type | solution.py:165
  7.2 91.5 %shard_map.28.blocks_ref = bf16[32,768,384]{2,1,0:T(8,128)(2,1)} custom-call(bf16[768,384]{1,0:T(8,128)(2,1)} %select_convert_fusion.own_ref), custom_call_target="tpu_custom_call" | custom-call | tf_op jit(solution)/shard_map/pallas_call | solution.py:428
  98.7 32.2 %shard_map.29 = bf16[768,384]{1,0:T(8,128)(2,1)} custom-call(s32[48,3]{1,0:T(8,128)S(1)} %copy.6.cells_ref, s32[8,3072]{1,0:T(8,128)S(1)} %scatter.4.lanes_ref, bf16[32,768,384]{2,1,0:T(8,128)(2,1)} %shard_map.28.blocks_ref), custom_call_target="tpu_custom_call" | custom-call | tf_op jit(solution)/shard_map/pallas_call | solution.py:451
  (5 shorter events, 0.1 us)

commit v6 on v4

--- a/solution.py
+++ b/solution.py
@@ -396,13 +396,12 @@
 
     keep_own = pltpu.make_async_copy(own_ref, part(row_id, 0, None), local_sem)
     keep_own.start()
-    for turn in range(len(slots) + 2):
-        if turn < len(slots):
-            stage_own(slots[turn])
-        if 1 <= turn <= len(slots):
-            stage_relay(slots[turn - 1])
-        if turn >= 2:
-            stage_diag(slots[turn - 2])
+    groups = [[0]] + [[1 + step, 1 + far_slot + step] for step in range(far_slot)]
+    for turn in range(len(groups) + 2):
+        for lag, stage in enumerate((stage_own, stage_relay, stage_diag)):
+            if 0 <= turn - lag < len(groups):
+                for slot in groups[turn - lag]:
+                    stage(slot)
     for slot in slots:
         stage_end(slot)
     keep_own.wait()

time: 125 us -> 124 us (level); the launches traced: 123 us -> 124 us
  no operation moved by 1% of the time
where the time goes in v6:
time: 124 us
  Pallas kernels  116 us (94%)
  other arithmetic  3.65 us (3%)
  local copies, waits for them, and re-layouts  3.5 us (3%)
    pallas_call x1, Pallas kernels, gather_blocks(): pl.pallas_call(gather_kernel, out_shape=jax.ShapeDtypeStruct((count, rows...  84.3 us
    pallas_call x1, Pallas kernels, per_device_gather(): pl.pallas_call(purify_kernel, out_shape=jax.ShapeDtypeStruct((rows, cols)...  32.2 us
    convert_element_type x1, other arithmetic, masked_density(): return jnp.where(near <= NEAR, value, 0.0).astype(jnp.bfloat16)  3.64 us

profile of v6, /device:TPU:7, one launch (start us, length us, event | category | flops | bytes accessed | tf_op | source)
XLA Modules:
  0.0 123.6 jit_solution(16852770844286354704)
XLA Ops:
  0.0 0.8 constant_dynamic-slice_fusion.1
  0.8 0.8 constant_dynamic-slice_fusion
  1.5 0.1 broadcast_in_dim.22
  1.6 0.1 reshape.40
  1.7 0.1 broadcast_in_dim.21
  1.8 0.1 reshape.39
  1.9 0.8 copy.6.cells_ref
  2.7 0.8 broadcast_in_dim.20
  3.4 0.1 reshape.38
  3.5 3.6 %select_convert_fusion.own_ref = bf16[768,384]{1,0:T(8,128)(2,1)} fusion(bf16[768,384]{1,0:T(8,128)(2,1)} %param.4, s32[384]{0:T(512)S(1)} %iota_add_fusion.1, s32[384]{0:T(512)S(1)} %get-tuple-element.21, s32[768]{0:T(1024)S(1)} %get-tuple-element.18, s32[384]{0:T(512)S(1)} %get-tuple-element.22, s32[768]{0:T(1024)S(1)} %get-tuple-element.19, ...), kind=kLoop, calls=%fused_computation.9 | loop fusion | flops 7372800 | bytes 1198080 | tf_op jit(solution)/shard_map/convert_element_type | solution.py:165
  7.2 84.3 %shard_map.28.blocks_ref = bf16[32,768,384]{2,1,0:T(8,128)(2,1)} custom-call(bf16[768,384]{1,0:T(8,128)(2,1)} %select_convert_fusion.own_ref), custom_call_target="tpu_custom_call" | custom-call | tf_op jit(solution)/shard_map/pallas_call | solution.py:417
  91.4 32.2 %shard_map.29 = bf16[768,384]{1,0:T(8,128)(2,1)} custom-call(s32[48,3]{1,0:T(8,128)S(1)} %copy.6.cells_ref, s32[8,3072]{1,0:T(8,128)S(1)} %scatter.4.lanes_ref, bf16[32,768,384]{2,1,0:T(8,128)(2,1)} %shard_map.28.blocks_ref), custom_call_target="tpu_custom_call" | custom-call | tf_op jit(solution)/shard_map/pallas_call | solution.py:440
  (5 shorter events, 0.1 us)
